TPU v7x, 256 devices: a whole 4x4x8 slice. The times are simulated.
256 devices in a mesh: segment: 4 (over z_hi), mp: 16 (over y, x), dp: 4 (over z_lo, core).
Axes of the slice: x: 4, y: 4, z: 8 (z_hi: 4, z_lo: 2; z = z_hi * 2 + z_lo), core: 2. Of those that a mesh axis runs over, the one named last changes fastest.
Arguments:
- frames: bfloat16 [128, 128, 1536], P(('segment', 'dp'), 'mp'), may hold values from -6 to 6
- latent_init: bfloat16 [64, 1536], replicated, may hold values from -6 to 6
- norm_gains: bfloat16 [3, 1536], replicated, may hold values from 0.099609375 to 1.8984375
- res_query: bfloat16 [1536, 1536], P(None, 'mp'), may hold values from -0.15625 to 0.15625
- res_kv: bfloat16 [1536, 2, 1536], P(None, None, 'mp'), may hold values from -0.15625 to 0.15625
- res_out: bfloat16 [1536, 1536], replicated, may hold values from -0.15625 to 0.15625
- text: bfloat16 [4, 4, 768, 8192], P('segment', 'dp', None, 'mp'), may hold values from -6 to 6
- text_gain: bfloat16 [4, 8192], P('segment'), may hold values from 0.099609375 to 1.8984375
- w_query: bfloat16 [4, 8192, 8192], P('segment', 'dp', 'mp'), may hold values from -0.0625 to 0.0625
- w_kv: bfloat16 [4, 1536, 2, 8192], P('segment', 'dp', None, 'mp'), may hold values from -0.15625 to 0.15625
- xgate: float32 [4], P('segment'), may hold values from 0.3 to 1.2
- frame_counts: int32 [4, 4], P('segment', 'dp'), may hold values from 1 to 8
- frame_dest: int32 [128], replicated, may hold values from 0 to 127, each once
- cotangent: bfloat16 [4, 4, 768, 8192], P('segment', 'dp', None, 'mp'), may hold values from -6 to 6
Outputs:
- context: bfloat16 [4, 4, 768, 8192], P('segment', 'dp', None, 'mp')
- latent_grad: float32 [64, 128, 1536], P('mp', ('segment', 'dp'))
Inputs may be any that keep to these rules, and one draw needn't show every extreme that they name: frame_dest is a permutation of the slots; a slot is used by its destination sequence only if its frame number is below that sequence's frame count.
All inputs are finite; a program needn't handle non-finite values.
Results may differ from a plain program's by a relative error of at most 0.04.
Values may be sent and summed in bfloat16 or wider, within the bound.
No kernel may reach another device: no remote copies, remote signals or barrier semaphores. Data moves between devices by JAX's collectives and lax.ppermute only.
A program may use at most 128 MiB of HBM per device.

v0:
```python
import math
import jax
import jax.numpy as jnp
from jax import lax
from jax.sharding import PartitionSpec as P

HD = 128
E = 1536
RESAMPLE_HEAD_DIM = 96
LAT = 64
FMAX = 8


def layer_norm(inputs, gain_row):
    values = inputs.astype(jnp.float32)
    center = values - jnp.mean(values, axis=-1, keepdims=True)
    spread = jnp.mean(center * center, axis=-1, keepdims=True)
    return center * lax.rsqrt(spread + 1e-05) * gain_row.astype(jnp.float32)


def attend(query_matrix, key_value_block, live, gate):
    score_matrix = jnp.einsum(
        "rag,lag->arl", query_matrix, key_value_block[:, 0], preferred_element_type=jnp.float32
    ) / math.sqrt(query_matrix.shape[-1])
    score_matrix = jnp.where(live[None, None, :], score_matrix, -1e30)
    row_max = lax.stop_gradient(jnp.max(score_matrix, axis=-1, keepdims=True))
    unnormalized_weights = jnp.exp(score_matrix - row_max)
    row_sum = jnp.sum(unnormalized_weights, axis=-1)
    blended_values = jnp.einsum(
        "lfv,vla->fla",
        unnormalized_weights.astype(jnp.bfloat16),
        key_value_block[:, 1],
        preferred_element_type=jnp.float32,
    )
    blended_values = blended_values / jnp.transpose(row_sum)[:, :, None]
    return gate * blended_values.reshape(blended_values.shape[0], -1)


def per_device(
    frames,
    latent_init,
    norm_gains,
    res_query,
    res_kv,
    res_out,
    text,
    text_gain,
    w_query,
    w_kv,
    xgate,
    frame_counts,
    frame_dest,
    cotangent,
):
    mp_count = lax.axis_size("mp")
    share = LAT // mp_count
    slots = frame_dest.shape[0]
    owned = frames.shape[0]
    res_cols = res_query.shape[1]
    res_local = res_cols // RESAMPLE_HEAD_DIM
    res_scale = 1.0 / math.sqrt(RESAMPLE_HEAD_DIM)
    lat_norm = layer_norm(latent_init, norm_gains[1]).astype(jnp.bfloat16)
    resampler_heads = (
        jnp.dot(lat_norm, res_query, preferred_element_type=jnp.float32)
        .astype(jnp.bfloat16)
        .reshape(LAT, res_local, RESAMPLE_HEAD_DIM)
    )
    latent_pair_rows = (
        jnp.einsum("le,ekc->lkc", lat_norm, res_kv, preferred_element_type=jnp.float32)
        .astype(jnp.bfloat16)
        .reshape(LAT, 2, res_local, RESAMPLE_HEAD_DIM)
    )
    first_scores = (
        jnp.einsum(
            "epg,apg->pea",
            resampler_heads,
            latent_pair_rows[:, 0],
            preferred_element_type=jnp.float32,
        )
        * res_scale
    )
    first_max = jnp.max(first_scores, axis=-1)
    first_exp = jnp.exp(first_scores - first_max[:, :, None])
    first_sum = jnp.sum(first_exp, axis=-1)
    first_acc = jnp.einsum(
        "nvf,fnr->nvr",
        first_exp.astype(jnp.bfloat16),
        latent_pair_rows[:, 1],
        preferred_element_type=jnp.float32,
    )
    piece = lax.all_gather(frames, "mp", axis=1, tiled=True)
    run_max = jnp.broadcast_to(first_max, (owned,) + first_max.shape)
    run_sum = jnp.broadcast_to(first_sum, (owned,) + first_sum.shape)
    run_acc = jnp.broadcast_to(first_acc, (owned,) + first_acc.shape)
    width = piece.shape[1]
    media = layer_norm(piece, norm_gains[0]).astype(jnp.bfloat16)
    media_pairs = (
        jnp.einsum("fpe,ekc->fpkc", media, res_kv, preferred_element_type=jnp.float32)
        .astype(jnp.bfloat16)
        .reshape(owned, width, 2, res_local, RESAMPLE_HEAD_DIM)
    )
    score_matrix = (
        jnp.einsum(
            "lhd,fphd->fhlp",
            resampler_heads,
            media_pairs[:, :, 0],
            preferred_element_type=jnp.float32,
        )
        * res_scale
    )
    new_max = jnp.maximum(run_max, jnp.max(score_matrix, axis=-1))
    fade = jnp.exp(run_max - new_max)
    unnormalized_weights = jnp.exp(score_matrix - new_max[..., None])
    new_sum = run_sum * fade + jnp.sum(unnormalized_weights, axis=-1)
    new_acc = run_acc * fade[..., None] + jnp.einsum(
        "fhlp,fphd->fhld",
        unnormalized_weights.astype(jnp.bfloat16),
        media_pairs[:, :, 1],
        preferred_element_type=jnp.float32,
    )
    res_context = (new_acc / new_sum[..., None]).astype(jnp.bfloat16)
    out_rows = lax.dynamic_slice_in_dim(res_out, lax.axis_index("mp") * res_cols, res_cols, 0)
    out_heads = out_rows.reshape(res_local, RESAMPLE_HEAD_DIM, E)
    part = res_context
    update = lax.psum_scatter(
        jnp.einsum("fhlr,hre->lfe", part, out_heads, preferred_element_type=jnp.float32).astype(
            jnp.bfloat16
        ),
        "mp",
        scatter_dimension=0,
        tiled=True,
    ).astype(jnp.float32)
    base_rows = lax.dynamic_slice_in_dim(
        latent_init, lax.axis_index("mp") * share, share, 0
    ).astype(jnp.float32)
    latents = layer_norm(base_rows[:, None, :] + update, norm_gains[2]).astype(jnp.bfloat16)
    gathered = lax.all_gather(latents, ("segment", "dp"), axis=1, tiled=True)
    group = lax.axis_index(("segment", "dp"))
    wanted = group * owned + jnp.arange(owned, dtype=jnp.int32)
    picker = (frame_dest[None, :] == wanted[:, None]).astype(jnp.bfloat16)
    mine = jnp.einsum("js,rse->rje", picker, gathered, preferred_element_type=jnp.float32).astype(
        jnp.bfloat16
    )
    dest = lax.all_gather(mine, "mp", axis=0, tiled=True)
    whole_text = lax.all_gather(text[0], "mp", axis=2, tiled=True)
    seq_local = whole_text.shape[0]
    txt_len = whole_text.shape[1]
    tokens = seq_local * txt_len
    text_norm = (
        layer_norm(whole_text, text_gain[0])
        .astype(jnp.bfloat16)
        .reshape(tokens, whole_text.shape[2])
    )
    head_cols = w_query.shape[2]
    head_local = head_cols // HD
    query_sum = jnp.dot(
        text_norm,
        lax.all_gather(w_query[0], "dp", axis=0, tiled=True),
        preferred_element_type=jnp.float32,
    )
    query_matrix = query_sum.astype(jnp.bfloat16).reshape(seq_local, txt_len, head_local, HD)
    full_kv = lax.all_gather(w_kv[0], "dp", axis=0, tiled=True)
    pair_sum = jnp.einsum("lje,ekc->jlkc", dest, full_kv, preferred_element_type=jnp.float32)
    pair_list = pair_sum.astype(jnp.bfloat16).reshape(seq_local, FMAX * LAT, 2, head_local, HD)
    live = jnp.repeat(
        jnp.arange(FMAX, dtype=jnp.int32)[None, :] < frame_counts[0][:, None], LAT, axis=1
    )
    gate = jnp.tanh(xgate[0])

    def local_attend(pair_in):
        return jax.vmap(attend, in_axes=(0, 0, 0, None))(query_matrix, pair_in, live, gate)

    gated, pull = jax.vjp(local_attend, pair_list)
    context = gated.astype(jnp.bfloat16)[None]
    (pair_grad,) = pull(cotangent[0].astype(jnp.float32))
    pair_grad = pair_grad.reshape(owned, LAT, 2, head_cols)
    part = pair_grad
    dest_grad = lax.psum_scatter(
        jnp.einsum("jlkc,ekc->lje", part, full_kv, preferred_element_type=jnp.float32).astype(
            jnp.bfloat16
        ),
        "mp",
        scatter_dimension=0,
        tiled=True,
    ).astype(jnp.float32)
    every_grad = lax.all_gather(
        dest_grad.astype(jnp.bfloat16), ("segment", "dp"), axis=1, tiled=True
    ).astype(dest_grad.dtype)
    targets = lax.dynamic_slice_in_dim(frame_dest, group * owned, owned, 0)
    chooser = (jnp.arange(slots, dtype=jnp.int32)[None, :] == targets[:, None]).astype(jnp.float32)
    latent_grad = jnp.einsum("js,rse->rje", chooser, every_grad, precision=lax.Precision.HIGHEST)
    return (context, latent_grad)


def solution(mesh):
    in_specs = (
        P(("segment", "dp"), "mp", None),
        P(),
        P(),
        P(None, "mp"),
        P(None, None, "mp"),
        P(),
        P("segment", "dp", None, "mp"),
        P("segment", None),
        P("segment", "dp", "mp"),
        P("segment", "dp", None, "mp"),
        P("segment"),
        P("segment", "dp"),
        P(),
        P("segment", "dp", None, "mp"),
    )
    out_specs = (P("segment", "dp", None, "mp"), P("mp", ("segment", "dp"), None))
    return jax.shard_map(
        per_device, mesh=mesh, in_specs=in_specs, out_specs=out_specs, check_vma=False
    )
```

profile of v0, /device:TPU:1, one launch (start us, length us, event | category | flops | bytes accessed | tf_op | source)
XLA Modules:
  0.0 658.1 jit_solution(9813244482838572930)
XLA Ops:
  7.2 0.7 all-gather.11.cloned.1.call-update
  8.0 0.9 convert_reduce_fusion.3
  8.8 1.1 convert_reduce_fusion.2
  9.9 1.2 fusion.108
  11.1 1.3 fusion.99
  12.4 1.3 convolution_convert_fusion.3
  14.1 52.8 %all-gather.11.cloned.1.call-done = bf16[8,128,1536]{2,1,0:T(8,128)(2,1)} async-done(((bf16[8,8,1536]{2,1,0:T(8,128)(2,1)}), bf16[8,128,1536]{2,1,0:T(8,128)(2,1)}) %all-gather.11.cloned.1.call-update) | async-done | bytes 3145744 | tf_op jit(solution)/shard_map/all_gather | solution.py:91
  66.9 2.5 convert_reduce_fusion.1
  69.5 2.8 fusion.15
  72.3 1.5 fusion.93
  74.4 1.7 fusion.43
  76.2 2.0 copy.37
  78.3 0.8 dynamic-slice_convert_fusion
  79.0 75.6 %reduce-scatter.3.cloned.1.call-done = bf16[4,8,1536]{2,1,0:T(8,128)(2,1)} async-done(((bf16[64,8,1536]{2,1,0:T(8,128)(2,1)}), bf16[4,8,1536]{2,1,0:T(8,128)(2,1)}) %reduce-scatter.3.cloned.1.call-update) | async-done | bytes 98320 | tf_op jit(solution)/shard_map/reduce_scatter | solution.py:125
  154.6 1.0 fusion.118
  155.6 1.1 multiply_reduce_fusion
  156.7 1.0 multiply_convert_fusion
  157.7 0.7 copy.38
  158.4 2.1 copy.40
  160.6 38.4 %all-gather.13.cloned.1.call-done = bf16[4,128,1536]{2,0,1:T(4,128)(2,1)} async-done(((bf16[4,8,1536]{2,0,1:T(4,128)(2,1)}), bf16[4,128,1536]{2,0,1:T(4,128)(2,1)}) %all-gather.13.cloned.1.call-update) | async-done | bytes 1572880 | tf_op jit(solution)/shard_map/all_gather | solution.py:137
  199.0 2.4 fusion.49
  201.5 0.5 all-gather.21.cloned.1.call-update
  202.1 0.7 all-gather.23.cloned.1.call-update
  203.8 1.7 copy.46
  206.3 34.1 %all-gather.19.cloned.1.call-done = bf16[1,1536,2,512]{3,1,2,0:T(8,128)(2,1)} async-done(((bf16[1,384,2,512]{3,1,2,0:T(8,128)(2,1)}), bf16[1,1536,2,512]{3,1,2,0:T(8,128)(2,1)}) %all-gather.19.cloned.1.call-update) | async-done | bytes 3145744 | tf_op jit(solution)/shard_map/all_gather | solution.py:162
  240.4 50.8 %all-gather.15.cloned.1.call-done = bf16[64,8,1536]{2,1,0:T(8,128)(2,1)} async-done(((bf16[4,8,1536]{2,1,0:T(8,128)(2,1)}), bf16[64,8,1536]{2,1,0:T(8,128)(2,1)}) %all-gather.15.cloned.1.call-update) | async-done | bytes 1572880 | tf_op jit(solution)/shard_map/all_gather | solution.py:144
  291.2 4.1 fusion.69
  295.3 0.6 copy.41
  295.9 0.5 reshape.414
  296.4 0.4 fusion.148
  297.1 100.5 %all-gather.21.cloned.1.call-done = bf16[1,1,768,8192]{3,2,1,0:T(8,128)(2,1)} async-done(((bf16[1,1,768,512]{3,2,1,0:T(8,128)(2,1)}), bf16[1,1,768,8192]{3,2,1,0:T(8,128)(2,1)}) %all-gather.21.cloned.1.call-update) | async-done | bytes 12582928 | tf_op jit(solution)/shard_map/all_gather | solution.py:145
  397.7 6.4 convert_reduce_fusion
  404.0 8.0 %fusion.3 = f32[768]{0:T(1024)S(1)} fusion(bf16[1,1,768,8192]{3,2,1,0:T(8,128)(2,1)} %all-gather.21.cloned.1.call-done, f32[768]{0:T(1024)S(1)} %broadcast_multiply_fusion), kind=kLoop, calls=%fused_computation.5 | loop fusion | flops 25165056 | bytes 12589056 | tf_op jit(solution)/shard_map/reduce_sum | solution.py:17
  412.0 72.3 %all-gather.23.cloned.1.call-done = bf16[1,8192,512]{2,1,0:T(8,128)(2,1)} async-done(((bf16[1,2048,512]{2,1,0:T(8,128)(2,1)}), bf16[1,8192,512]{2,1,0:T(8,128)(2,1)}) %all-gather.23.cloned.1.call-update) | async-done | bytes 8388624 | tf_op jit(solution)/shard_map/all_gather | solution.py:158
  484.3 17.6 %fusion.64 = bf16[768,512]{0,1:T(8,128)(2,1)S(1)} fusion(bf16[1,8192,512]{2,1,0:T(8,128)(2,1)} %all-gather.23.cloned.1.call-done, bf16[1,1,768,8192]{3,2,1,0:T(8,128)(2,1)} %all-gather.21.cloned.1.call-done, f32[8192]{0:T(1024)S(1)} %bitcast.222, f32[768]{0:T(1024)S(1)} %add_rsqrt_fusion, f32[768]{0:T(1024)S(1)} %broadcast_multiply_fusion), kind=kOutput, calls=%fused_computation.65 | convolution fusion | flops 6474301440 | bytes 21796864 | tf_op jit(solution)/shard_map/dot_general | solution.py:156
  501.8 1.1 fusion.24
  502.9 1.4 fusion.25
  504.4 1.7 fusion.90
  506.2 2.8 fusion.53
  508.9 7.0 %fusion.85 = bf16[1,512,1,4,128]{1,4,3,2,0:T(8,128)(2,1)} fusion(bf16[768,4,128]{0,2,1:T(8,128)(2,1)S(1)} %bitcast.217, f32[4,768,512]{1,2,0:T(8,128)} %copy-done.2, f32[4,768]{1,0:T(4,128)S(1)} %negate_bitcast_fusion, f32[4,768]{1,0:T(4,128)S(1)} %get-tuple-element.21, pred[512]{0:T(512)(128)(4,1)S(1)} %broadcast_in_dim.37, ...), kind=kOutput, calls=%fused_computation.70 | convolution fusion | flops 820117504 | bytes 9736704 | tf_op jit(solution)/shard_map/transpose(jvp(vmap(rag,lag->arl)))/dot_general | solution.py:22
  516.0 2.1 pad_add_fusion
  518.1 2.8 reshape.439
  520.9 3.4 copy.54
  524.2 5.3 fusion.44
  529.6 77.0 %reduce-scatter.5.cloned.1.call-done = bf16[4,8,1536]{2,1,0:T(8,128)(2,1)} async-done(((bf16[64,8,1536]{2,1,0:T(8,128)(2,1)}), bf16[4,8,1536]{2,1,0:T(8,128)(2,1)}) %reduce-scatter.5.cloned.1.call-update) | async-done | bytes 98320 | tf_op jit(solution)/shard_map/reduce_scatter | solution.py:178
  606.7 1.2 copy.55
  607.9 41.2 %all-gather.17.cloned.1.call-done = bf16[4,128,1536]{2,1,0:T(8,128)(2,1)} async-done(((bf16[4,8,1536]{2,1,0:T(8,128)(2,1)}), bf16[4,128,1536]{2,1,0:T(8,128)(2,1)}) %all-gather.17.cloned.1.call-update) | async-done | bytes 1572880 | tf_op jit(solution)/shard_map/all_gather | solution.py:186
  649.1 2.5 convolution_bitcast_fusion.1
  (58 shorter events, 2.3 us)
Async XLA Ops:
  7.2 3.9 copy-start
  7.2 59.8 %all-gather.11.cloned.1.call-start = ((), (), s32[]{:S(2)}) async-start(), calls=%async_computation.2 | async-start | bytes 3342336 | tf_op jit(solution)/shard_map/all_gather | solution.py:91
  7.9 146.7 %reduce-scatter.3.cloned.1.call-start = ((), (), s32[]{:S(2)}) async-start(), calls=%async_computation.3 | async-start | bytes 1671168 | tf_op jit(solution)/shard_map/reduce_scatter | solution.py:125
  66.9 5.4 copy-start.3
  73.8 125.2 %copy-start.8 = (s32[128]{0:T(128)S(1)}, s32[128]{0:T(128)}, u32[]{:S(2)}) copy-start(s32[128]{0:T(128)} %param.26) | copy-start | bytes 1540
  76.2 127.4 %copy-start.5 = (bf16[1,1,768,512]{3,2,1,0:T(8,128)(2,1)S(1)}, bf16[1,1,768,512]{3,2,1,0:T(8,128)(2,1)}, u32[]{:S(2)}) copy-start(bf16[1,1,768,512]{3,2,1,0:T(8,128)(2,1)} %param.27) | copy-start | bytes 2359300
  78.2 120.8 %all-gather.13.cloned.1.call-start = ((), (), s32[]{:S(2)}) async-start(), calls=%async_computation.4 | async-start | bytes 1671168 | tf_op jit(solution)/shard_map/all_gather | solution.py:137
  158.4 47.9 %copy-start.7 = (bf16[1,8192]{1,0:T(2,128)(2,1)S(1)}, bf16[1,8192]{1,0:T(2,128)(2,1)}, u32[]{:S(2)}) copy-start(bf16[1,8192]{1,0:T(2,128)(2,1)} %param.21) | copy-start | bytes 49156
  158.4 82.0 %all-gather.19.cloned.1.call-start = ((), (), s32[]{:S(2)}) async-start(), calls=%async_computation.8 | async-start | bytes 3932160 | tf_op jit(solution)/shard_map/all_gather | solution.py:162
  160.6 130.6 %all-gather.15.cloned.1.call-start = ((), (), s32[]{:S(2)}) async-start(), calls=%async_computation.5 | async-start | bytes 1671168 | tf_op jit(solution)/shard_map/all_gather | solution.py:144
  201.5 196.2 %all-gather.21.cloned.1.call-start = ((), (), s32[]{:S(2)}) async-start(), calls=%async_computation.9 | async-start | bytes 13369344 | tf_op jit(solution)/shard_map/all_gather | solution.py:145
  202.1 282.2 %all-gather.23.cloned.1.call-start = ((), (), s32[]{:S(2)}) async-start(), calls=%async_computation.10 | async-start | bytes 10485760 | tf_op jit(solution)/shard_map/all_gather | solution.py:158
  202.8 403.8 %reduce-scatter.5.cloned.1.call-start = ((), (), s32[]{:S(2)}) async-start(), calls=%async_computation.6 | async-start | bytes 1671168 | tf_op jit(solution)/shard_map/reduce_scatter | solution.py:178
  501.8 2.6 copy-start.4
  502.9 3.2 copy-start.2
  524.2 82.5 %copy-start.6 = (bf16[1,768,4,128]{1,3,2,0:T(8,128)(2,1)S(1)}, bf16[1,768,4,128]{1,3,2,0:T(8,128)(2,1)}, u32[]{:S(2)}) copy-start(bf16[1,768,4,128]{1,3,2,0:T(8,128)(2,1)} %get-tuple-element.14) | copy-start | bytes 2359300
  524.2 127.3 %copy-start.1 = (bf16[1536,2,96]{0,2,1:T(8,128)(2,1)S(1)}, bf16[1536,2,96]{0,2,1:T(8,128)(2,1)}, u32[]{:S(2)}) copy-start(bf16[1536,2,96]{0,2,1:T(8,128)(2,1)} %param.18) | copy-start | bytes 1769476
  529.6 119.5 %all-gather.17.cloned.1.call-start = ((), (), s32[]{:S(2)}) async-start(), calls=%async_computation.7 | async-start | bytes 1671168 | tf_op jit(solution)/shard_map/all_gather | solution.py:186
Sparse Core Ops, SparseCore 0:
  10.4 56.4 all-gather.10
  78.3 76.1 reduce-scatter.2
  158.5 40.4 all-gather.12
  201.3 39.1 all-gather.18
  243.3 47.8 all-gather.14
  293.5 104.1 all-gather.20
  399.5 84.7 all-gather.22
  529.7 76.8 reduce-scatter.4
  608.5 40.5 all-gather.16
where the time goes:
time: 659 us; the launch traced here: 658 us
  waiting for transfers between devices  545 us (83%)
  matrix products  50.9 us (8%)
  other arithmetic  30.7 us (5%)
  local copies, waits for them, and re-layouts  15.8 us (2%)
  between operations  15.5 us (2%)
    all_gather x1, waiting for transfers between devices, per_device(): whole_text = lax.all_gather(text[0], 'mp', axis=2, tiled=True)  101 us
    reduce_scatter x1, waiting for transfers between devices, per_device(): lax.psum_scatter(jnp.einsum('jlkc,ekc->lje', part, full_kv, preferred_ele...  77 us
    reduce_scatter x1, waiting for transfers between devices, per_device(): lax.psum_scatter(jnp.einsum('fhlr,hre->lfe', part, out_heads, preferred_e...  75.6 us
    all_gather x1, waiting for transfers between devices, per_device(): lax.all_gather(w_query[0], 'dp', axis=0, tiled=True)  72.3 us
    all_gather x1, waiting for transfers between devices, per_device(): piece = lax.all_gather(frames, 'mp', axis=1, tiled=True)  52.8 us
    all_gather x1, waiting for transfers between devices, per_device(): dest = lax.all_gather(mine, 'mp', axis=0, tiled=True)  50.8 us
    all_gather x1, waiting for transfers between devices, per_device(): lax.all_gather(dest_grad.astype(jnp.bfloat16), ('segment', 'dp'), axis=1,...  41.2 us
    all_gather x1, waiting for transfers between devices, per_device(): gathered = lax.all_gather(latents, ('segment', 'dp'), axis=1, tiled=True)  38.4 us
  transfers between devices with their start and end apart: 9, of which 9 were waited for; matrix products, arithmetic and copies ran while one was open for 5% of the time, Pallas kernels for 0%

commit v1 on v0

--- a/solution.py
+++ b/solution.py
@@ -159,7 +159,9 @@
         preferred_element_type=jnp.float32,
     )
     query_matrix = query_sum.astype(jnp.bfloat16).reshape(seq_local, txt_len, head_local, HD)
-    full_kv = lax.all_gather(w_kv[0], "dp", axis=0, tiled=True)
+    full_kv = jnp.concatenate(
+        lax.all_to_all(jnp.stack([w_kv[0]] * lax.axis_size("dp")), "dp", 0, 0), axis=0
+    )
     pair_sum = jnp.einsum("lje,ekc->jlkc", dest, full_kv, preferred_element_type=jnp.float32)
     pair_list = pair_sum.astype(jnp.bfloat16).reshape(seq_local, FMAX * LAT, 2, head_local, HD)
     live = jnp.repeat(

time: 659 us -> 616 us (0.935)
  waiting for transfers between devices: 545 us -> 492 us
    all_gather x1, waiting for transfers between devices: 50.8 us -> 0.01 us  [per_device(): dest = lax.all_gather(mine, 'mp', axis=0, tiled=True)]
    all_gather x1 -> x0, waiting for transfers between devices: 34.1 us -> none  [per_device(): full_kv = lax.all_gather(w_kv[0], 'dp', axis=0, tiled=True)]
    all_to_all x0 -> x1, waiting for transfers between devices: none -> 32.7 us  [per_device(): lax.all_to_all(jnp.stack([w_kv[0]] * lax.axis_size('dp')), 'dp', 0, 0)]
  transfers between devices with their start and end apart: 9 -> 9, of which waited for: 9 -> 8; matrix products, arithmetic and copies ran while one was open for 5% -> 6% of each run, Pallas kernels for 0% -> 0%
where the time goes in v1:
time: 616 us; the launch traced here: 615 us
  waiting for transfers between devices  492 us (80%)
  matrix products  50.9 us (8%)
  other arithmetic  30.7 us (5%)
  local copies, waits for them, and re-layouts  20.8 us (3%)
  between operations  15.8 us (3%)
    all_gather x1, waiting for transfers between devices, per_device(): whole_text = lax.all_gather(text[0], 'mp', axis=2, tiled=True)  98 us
    reduce_scatter x1, waiting for transfers between devices, per_device(): lax.psum_scatter(jnp.einsum('jlkc,ekc->lje', part, full_kv, preferred_ele...  77 us
    reduce_scatter x1, waiting for transfers between devices, per_device(): lax.psum_scatter(jnp.einsum('fhlr,hre->lfe', part, out_heads, preferred_e...  75.6 us
    all_gather x1, waiting for transfers between devices, per_device(): lax.all_gather(w_query[0], 'dp', axis=0, tiled=True)  72.1 us
    all_gather x1, waiting for transfers between devices, per_device(): piece = lax.all_gather(frames, 'mp', axis=1, tiled=True)  52.8 us
    all_gather x1, waiting for transfers between devices, per_device(): lax.all_gather(dest_grad.astype(jnp.bfloat16), ('segment', 'dp'), axis=1,...  41.2 us
    all_gather x1, waiting for transfers between devices, per_device(): gathered = lax.all_gather(latents, ('segment', 'dp'), axis=1, tiled=True)  40.7 us
    all_to_all x1, waiting for transfers between devices, per_device(): lax.all_to_all(jnp.stack([w_kv[0]] * lax.axis_size('dp')), 'dp', 0, 0)  32.7 us
  transfers between devices with their start and end apart: 9, of which 8 were waited for; matrix products, arithmetic and copies ran while one was open for 6% of the time, Pallas kernels for 0%

profile of v1, /device:TPU:1, one launch (start us, length us, event | category | flops | bytes accessed | tf_op | source)
XLA Modules:
  0.0 615.4 jit_solution(7815290016087576695)
XLA Ops:
  7.2 0.7 all-gather.9.cloned.1.call-update
  8.0 0.9 convert_reduce_fusion.3
  8.8 1.1 convert_reduce_fusion.2
  9.9 1.2 fusion.98
  11.1 1.3 fusion.89
  12.4 1.3 convolution_convert_fusion.3
  14.1 52.8 %all-gather.9.cloned.1.call-done = bf16[8,128,1536]{2,1,0:T(8,128)(2,1)} async-done(((bf16[8,8,1536]{2,1,0:T(8,128)(2,1)}), bf16[8,128,1536]{2,1,0:T(8,128)(2,1)}) %all-gather.9.cloned.1.call-update) | async-done | bytes 3145744 | tf_op jit(solution)/shard_map/all_gather | solution.py:91
  66.9 2.5 convert_reduce_fusion.1
  69.5 2.8 fusion.15
  72.3 1.5 fusion.83
  74.4 1.7 fusion.38
  76.1 2.0 copy.37
  78.2 0.8 dynamic-slice_convert_fusion
  79.0 75.6 %reduce-scatter.3.cloned.1.call-done = bf16[4,8,1536]{2,1,0:T(8,128)(2,1)} async-done(((bf16[64,8,1536]{2,1,0:T(8,128)(2,1)}), bf16[4,8,1536]{2,1,0:T(8,128)(2,1)}) %reduce-scatter.3.cloned.1.call-update) | async-done | bytes 98320 | tf_op jit(solution)/shard_map/reduce_scatter | solution.py:125
  154.6 1.0 fusion.108
  155.6 1.1 multiply_reduce_fusion
  156.7 1.0 multiply_convert_fusion
  157.7 0.7 copy.38
  158.4 40.7 %all-gather.11.cloned.1.call-done = bf16[4,128,1536]{2,0,1:T(4,128)(2,1)} async-done(((bf16[4,8,1536]{2,0,1:T(4,128)(2,1)}), bf16[4,128,1536]{2,0,1:T(4,128)(2,1)}) %all-gather.11.cloned.1.call-update) | async-done | bytes 1572880 | tf_op jit(solution)/shard_map/all_gather | solution.py:137
  199.1 2.4 fusion.42
  201.6 0.5 all-gather.17.cloned.1.call-update
  202.2 0.5 all-gather.19.cloned.1.call-update
  202.7 1.3 copy.40
  204.0 1.9 stack.3
  206.0 5.0 all-to-all-start
  211.9 1.7 copy.47
  214.4 32.7 %all-to-all-done = bf16[4,384,2,512]{3,1,2,0:T(8,128)(2,1)} async-done(((bf16[4,384,2,512]{3,1,2,0:T(8,128)(2,1)}), bf16[4,384,2,512]{3,1,2,0:T(8,128)(2,1)}, u32[]{:S(2)}, u32[]{:S(2)}) %all-to-all-start) | async-done | bytes 3145760 | tf_op jit(solution)/shard_map/all_to_all | solution.py:163
  247.1 3.8 copy.41
  250.9 4.1 fusion.61
  255.0 0.6 copy.42
  256.8 98.0 %all-gather.17.cloned.1.call-done = bf16[1,1,768,8192]{3,2,1,0:T(8,128)(2,1)} async-done(((bf16[1,1,768,512]{3,2,1,0:T(8,128)(2,1)}), bf16[1,1,768,8192]{3,2,1,0:T(8,128)(2,1)}) %all-gather.17.cloned.1.call-update) | async-done | bytes 12582928 | tf_op jit(solution)/shard_map/all_gather | solution.py:145
  354.8 6.4 %convert_reduce_fusion = f32[768]{0:T(1024)S(1)} fusion(bf16[1,1,768,8192]{3,2,1,0:T(8,128)(2,1)} %all-gather.17.cloned.1.call-done), kind=kLoop, calls=%fused_computation | loop fusion | flops 12582144 | bytes 12585984 | tf_op jit(solution)/shard_map/reduce_sum | solution.py:16
  361.1 8.0 %fusion.3 = f32[768]{0:T(1024)S(1)} fusion(bf16[1,1,768,8192]{3,2,1,0:T(8,128)(2,1)} %all-gather.17.cloned.1.call-done, f32[768]{0:T(1024)S(1)} %broadcast_multiply_fusion), kind=kLoop, calls=%fused_computation.5 | loop fusion | flops 25165056 | bytes 12589056 | tf_op jit(solution)/shard_map/reduce_sum | solution.py:17
  369.1 72.1 %all-gather.19.cloned.1.call-done = bf16[1,8192,512]{2,1,0:T(8,128)(2,1)} async-done(((bf16[1,2048,512]{2,1,0:T(8,128)(2,1)}), bf16[1,8192,512]{2,1,0:T(8,128)(2,1)}) %all-gather.19.cloned.1.call-update) | async-done | bytes 8388624 | tf_op jit(solution)/shard_map/all_gather | solution.py:158
  441.2 17.6 %fusion.56 = bf16[768,512]{0,1:T(8,128)(2,1)S(1)} fusion(bf16[1,8192,512]{2,1,0:T(8,128)(2,1)} %all-gather.19.cloned.1.call-done, bf16[1,1,768,8192]{3,2,1,0:T(8,128)(2,1)} %all-gather.17.cloned.1.call-done, f32[8192]{0:T(1024)S(1)} %bitcast.217, f32[768]{0:T(1024)S(1)} %add_rsqrt_fusion, f32[768]{0:T(1024)S(1)} %broadcast_multiply_fusion), kind=kOutput, calls=%fused_computation.63 | convolution fusion | flops 6474301440 | bytes 21796864 | tf_op jit(solution)/shard_map/dot_general | solution.py:156
  458.8 1.1 fusion.24
  459.9 1.4 fusion.25
  461.4 1.7 fusion.80
  463.1 2.8 fusion.47
  465.9 7.0 %fusion.75 = bf16[1,512,1,4,128]{1,4,3,2,0:T(8,128)(2,1)} fusion(bf16[768,4,128]{0,2,1:T(8,128)(2,1)S(1)} %bitcast.211, f32[4,768,512]{1,2,0:T(8,128)} %copy-done.2, f32[4,768]{1,0:T(4,128)S(1)} %negate_bitcast_fusion, f32[4,768]{1,0:T(4,128)S(1)} %get-tuple-element.21, pred[512]{0:T(512)(128)(4,1)S(1)} %broadcast_in_dim.37, ...), kind=kOutput, calls=%fused_computation.68 | convolution fusion | flops 820117504 | bytes 9736704 | tf_op jit(solution)/shard_map/transpose(jvp(vmap(rag,lag->arl)))/dot_general | solution.py:22
  472.9 2.1 pad_add_fusion
  475.0 2.8 reshape.443
  477.8 3.4 copy.55
  481.2 5.3 fusion.39
  486.6 77.0 %reduce-scatter.5.cloned.1.call-done = bf16[4,8,1536]{2,1,0:T(8,128)(2,1)} async-done(((bf16[64,8,1536]{2,1,0:T(8,128)(2,1)}), bf16[4,8,1536]{2,1,0:T(8,128)(2,1)}) %reduce-scatter.5.cloned.1.call-update) | async-done | bytes 98320 | tf_op jit(solution)/shard_map/reduce_scatter | solution.py:180
  563.7 1.2 copy.56
  564.9 41.2 %all-gather.15.cloned.1.call-done = bf16[4,128,1536]{2,1,0:T(8,128)(2,1)} async-done(((bf16[4,8,1536]{2,1,0:T(8,128)(2,1)}), bf16[4,128,1536]{2,1,0:T(8,128)(2,1)}) %all-gather.15.cloned.1.call-update) | async-done | bytes 1572880 | tf_op jit(solution)/shard_map/all_gather | solution.py:188
  606.1 2.5 convolution_bitcast_fusion.1
  (59 shorter events, 3.1 us)
Async XLA Ops:
  7.2 3.9 copy-start
  7.2 59.8 %all-gather.9.cloned.1.call-start = ((), (), s32[]{:S(2)}) async-start(), calls=%async_computation.3 | async-start | bytes 3342336 | tf_op jit(solution)/shard_map/all_gather | solution.py:91
  7.9 146.7 %reduce-scatter.3.cloned.1.call-start = ((), (), s32[]{:S(2)}) async-start(), calls=%async_computation.4 | async-start | bytes 1671168 | tf_op jit(solution)/shard_map/reduce_scatter | solution.py:125
  66.9 5.4 copy-start.3
  73.8 125.3 %copy-start.8 = (s32[128]{0:T(128)S(1)}, s32[128]{0:T(128)}, u32[]{:S(2)}) copy-start(s32[128]{0:T(128)} %param.26) | copy-start | bytes 1540
  78.2 120.9 %all-gather.11.cloned.1.call-start = ((), (), s32[]{:S(2)}) async-start(), calls=%async_computation.5 | async-start | bytes 1671168 | tf_op jit(solution)/shard_map/all_gather | solution.py:137
  158.4 92.5 %all-gather.13.cloned.1.call-start = ((), (), s32[]{:S(2)}) async-start(), calls=%async_computation.6 | async-start | bytes 1671168 | tf_op jit(solution)/shard_map/all_gather | solution.py:144
  201.5 153.2 %all-gather.17.cloned.1.call-start = ((), (), s32[]{:S(2)}) async-start(), calls=%async_computation.9 | async-start | bytes 13369344 | tf_op jit(solution)/shard_map/all_gather | solution.py:145
  202.1 239.1 %all-gather.19.cloned.1.call-start = ((), (), s32[]{:S(2)}) async-start(), calls=%async_computation.10 | async-start | bytes 10485760 | tf_op jit(solution)/shard_map/all_gather | solution.py:158
  202.7 8.9 %copy-start.5 = (bf16[1,1,768,512]{3,2,1,0:T(8,128)(2,1)S(1)}, bf16[1,1,768,512]{3,2,1,0:T(8,128)(2,1)}, u32[]{:S(2)}) copy-start(bf16[1,1,768,512]{3,2,1,0:T(8,128)(2,1)} %param.27) | copy-start | bytes 2359300
  206.0 8.4 %copy-start.7 = (bf16[1,8192]{1,0:T(2,128)(2,1)S(1)}, bf16[1,8192]{1,0:T(2,128)(2,1)}, u32[]{:S(2)}) copy-start(bf16[1,8192]{1,0:T(2,128)(2,1)} %param.21) | copy-start | bytes 49156
  206.0 41.1 %all-to-all-start = ((bf16[4,384,2,512]{3,1,2,0:T(8,128)(2,1)}), bf16[4,384,2,512]{3,1,2,0:T(8,128)(2,1)}, u32[]{:S(2)}, u32[]{:S(2)}) async-start(bf16[4,384,2,512]{3,1,2,0:T(8,128)(2,1)} %stack.3), calls=%async_computation.1 | async-start | bytes 6291456 | tf_op jit(solution)/shard_map/all_to_all | solution.py:163
  210.9 352.7 %reduce-scatter.5.cloned.1.call-start = ((), (), s32[]{:S(2)}) async-start(), calls=%async_computation.7 | async-start | bytes 1671168 | tf_op jit(solution)/shard_map/reduce_scatter | solution.py:180
  458.8 2.6 copy-start.4
  459.9 3.2 copy-start.2
  481.2 82.5 %copy-start.6 = (bf16[1,768,4,128]{1,3,2,0:T(8,128)(2,1)S(1)}, bf16[1,768,4,128]{1,3,2,0:T(8,128)(2,1)}, u32[]{:S(2)}) copy-start(bf16[1,768,4,128]{1,3,2,0:T(8,128)(2,1)} %get-tuple-element.14) | copy-start | bytes 2359300
  481.2 127.3 %copy-start.1 = (bf16[1536,2,96]{0,2,1:T(8,128)(2,1)S(1)}, bf16[1536,2,96]{0,2,1:T(8,128)(2,1)}, u32[]{:S(2)}) copy-start(bf16[1536,2,96]{0,2,1:T(8,128)(2,1)} %param.18) | copy-start | bytes 1769476
  486.5 119.5 %all-gather.15.cloned.1.call-start = ((), (), s32[]{:S(2)}) async-start(), calls=%async_computation.8 | async-start | bytes 1671168 | tf_op jit(solution)/shard_map/all_gather | solution.py:188
Sparse Core Ops, SparseCore 0:
  10.4 56.4 all-gather.8
  78.3 76.2 reduce-scatter.2
  158.5 40.5 all-gather.10
  202.0 46.3 all-gather.12
  250.6 104.1 all-gather.16
  356.4 84.7 all-gather.18
  486.7 76.9 reduce-scatter.4
  565.5 40.5 all-gather.14
